TPU v7x, 32 devices: a whole 2x2x4 slice. The times are simulated.
32 devices in a mesh: band: 16 (over z, y, x), mp: 2 (over core).
Axes of the slice: x: 2, y: 2, z: 4, core: 2. Of those that a mesh axis runs over, the one named last changes fastest.
Arguments:
- grid_nodes: bfloat16 [65536, 512], P('band', 'mp'), may hold values from -6 to 6
- mesh_nodes: bfloat16 [8192, 512], P('band', 'mp'), may hold values from -6 to 6
- send_weight: bfloat16 [512, 512], P(None, 'mp'), may hold values from -0.25 to 0.25
- self_weight: bfloat16 [512, 512], P(None, 'mp'), may hold values from -0.25 to 0.25
- pooled_weight: bfloat16 [512, 512], P(None, 'mp'), may hold values from -0.25 to 0.25
- out_weight: bfloat16 [512, 2, 512], P('mp'), may hold values from -0.25 to 0.25
- encode_source: int32 [3072], P('band'), may hold values from 0 to 31
- encode_slot: int32 [3072], P('band'), may hold values from 0 to 15
- encode_tiles: bfloat16 [3072, 128, 128], P('band'), may hold values from -0.078125 to 0.078125
- slot_block: int32 [16, 16], P('band'), may hold values from 0 to 3
- decode_slot: int32 [3072], P('band'), may hold values from 0 to 15
- decode_target: int32 [3072], P('band'), may hold values from 0 to 31
- decode_tiles: bfloat16 [3072, 128, 128], P('band'), may hold values from -0.21875 to 0.21875
Outputs:
- grid_state: bfloat16 [65536, 512], P('band', 'mp')
- mesh_state: bfloat16 [8192, 512], P('band', 'mp')
All inputs are finite; a program needn't handle non-finite values.
Results may differ from a plain program's by a relative error of at most 0.005.
Values may be sent and summed in bfloat16 or wider, within the bound.
A program may use at most 192 MiB of HBM per device.

v0:
```python
import jax
import jax.numpy as jnp
from jax import lax
from jax.sharding import PartitionSpec as P


def per_device(
    grid_nodes,
    mesh_nodes,
    send_weight,
    self_weight,
    pooled_weight,
    out_weight,
    encode_source,
    encode_slot,
    encode_tiles,
    slot_block,
    decode_slot,
    decode_target,
    decode_tiles,
):
    band_count = lax.axis_size("band")
    tile_edge = encode_tiles.shape[1]
    feature_width = grid_nodes.shape[1]
    grid_blocks = grid_nodes.shape[0] // tile_edge
    mesh_blocks = mesh_nodes.shape[0] // tile_edge
    full_grid = lax.all_gather(grid_nodes, "mp", axis=1, tiled=True)
    message = jax.nn.silu(
        jnp.dot(full_grid, send_weight, preferred_element_type=jnp.float32)
    ).astype(jnp.bfloat16)
    message_blocks = message.reshape(grid_blocks, tile_edge, feature_width)
    sources = jnp.take(message_blocks, encode_source, axis=0)
    partials = jnp.einsum("eij,ejc->eic", encode_tiles, sources, preferred_element_type=jnp.float32)
    slot_sums = jax.ops.segment_sum(partials, encode_slot, num_segments=band_count)
    arrived, owner_block = (
        lax.all_to_all(slot_sums, "band", split_axis=0, concat_axis=0, tiled=True),
        lax.all_to_all(slot_block[0], "band", split_axis=0, concat_axis=0, tiled=True),
    )
    selector = (owner_block[None, :] == jnp.arange(mesh_blocks, dtype=jnp.int32)[:, None]).astype(
        jnp.float32
    )
    aggregate = jnp.einsum("bs,sic->bic", selector, arrived, precision=lax.Precision.HIGHEST)
    pooled = aggregate.reshape(-1, feature_width).astype(jnp.bfloat16)
    mesh_full, pooled_full = (
        lax.all_gather(mesh_nodes, "mp", axis=1, tiled=True),
        lax.all_gather(pooled, "mp", axis=1, tiled=True),
    )
    inner_sum = jnp.dot(mesh_full, self_weight, preferred_element_type=jnp.float32) + jnp.dot(
        pooled_full, pooled_weight, preferred_element_type=jnp.float32
    )
    hidden = jax.nn.silu(inner_sum).astype(jnp.bfloat16)
    partial_out = jnp.dot(
        hidden, out_weight.reshape(hidden.shape[1], -1), preferred_element_type=jnp.float32
    )
    partial_out = partial_out.reshape(hidden.shape[0], 2, -1)
    reduced = lax.psum_scatter(partial_out, "mp", scatter_dimension=2, tiled=True)
    mesh_state = (mesh_nodes.astype(jnp.float32) + reduced[:, 0, :]).astype(jnp.bfloat16)
    decode_source = (
        reduced[:, 1, :].astype(jnp.bfloat16).reshape(mesh_blocks, tile_edge, feature_width)
    )
    outgoing = jnp.take(decode_source, owner_block, axis=0)
    returned = lax.all_to_all(outgoing, "band", split_axis=0, concat_axis=0, tiled=True)
    picked = jnp.take(returned, decode_slot, axis=0)
    contribution = jnp.einsum(
        "eij,ejc->eic", decode_tiles, picked, preferred_element_type=jnp.float32
    )
    grid_sum = jax.ops.segment_sum(contribution, decode_target, num_segments=grid_blocks)
    grid_state = (grid_nodes.astype(jnp.float32) + grid_sum.reshape(-1, feature_width)).astype(
        jnp.bfloat16
    )
    return (grid_state, mesh_state)


def solution(mesh):
    return jax.shard_map(
        per_device,
        mesh=mesh,
        in_specs=(
            P("band", "mp"),
            P("band", "mp"),
            P(None, "mp"),
            P(None, "mp"),
            P(None, "mp"),
            P("mp", None, None),
            P("band"),
            P("band"),
            P("band", None, None),
            P("band", None),
            P("band"),
            P("band"),
            P("band", None, None),
        ),
        out_specs=(P("band", "mp"), P("band", "mp")),
        check_vma=False,
    )
```

profile of v0, /device:TPU:8, one launch (start us, length us, event | category | flops | bytes accessed | tf_op | source)
XLA Modules:
  0.0 359.2 jit_solution(4791262341297748504)
XLA Ops:
  7.9 1.3 copy.31
  9.2 7.2 %all-to-all-start = ((s32[16,1,1]{2,1,0:T(1,128)}), s32[16,1,1]{2,1,0:T(1,128)S(1)}, u32[]{:S(2)}, u32[]{:S(2)}) async-start(s32[16,1,1]{2,1,0:T(1,128)} %copy.31), calls=%async_computation | async-start | bytes 16384 | tf_op jit(solution)/shard_map/all_to_all | solution.py:37
  17.9 6.2 %all-gather.2.cloned.1.call-done = bf16[4096,512]{1,0:T(8,128)(2,1)} async-done(((bf16[4096,256]{1,0:T(8,128)(2,1)}), bf16[4096,512]{1,0:T(8,128)(2,1)}) %all-gather.2.cloned.1.call-update) | async-done | bytes 4194320 | tf_op jit(solution)/shard_map/all_gather | solution.py:27
  24.0 3.4 multiply_convert_fusion
  27.5 8.3 %gather_fusion = bf16[192,128,256]{2,1,0:T(8,128)(2,1)} fusion(bf16[32,128,256]{2,1,0:T(8,128)(2,1)S(1)} %bitcast.43, s32[1024]{0:T(1024)S(1)} %pad_clamp_fusion.2), kind=kCustom, calls=%fused_computation | custom fusion | bytes 25166592 | tf_op jit(solution)/shard_map/jit(_take)/gather | solution.py:32
  35.8 16.4 %fusion.6 = f32[192,128,256]{1,2,0:T(8,128)} fusion(bf16[192,128,128]{2,1,0:T(8,128)(2,1)} %param.21, bf16[192,128,256]{2,1,0:T(8,128)(2,1)} %gather_fusion, pred[192]{0:T(512)(128)(4,1)S(1)} %compare_and_fusion), kind=kOutput, calls=%fused_computation.11 | convolution fusion | flops 1616904192 | bytes 44040384 | tf_op jit(solution)/shard_map/eij,ejc->eic/dot_general | solution.py:33
  52.1 24.6 %copy.33 = f32[192,128,256]{2,1,0:T(8,128)} copy(f32[192,128,256]{1,2,0:T(8,128)} %fusion.6) | data formatting | bytes 50331648 | tf_op jit(solution)/shard_map/eij,ejc->eic/dot_general | solution.py:33
  76.8 1.5 broadcast_in_dim.50
  78.3 54.0 %scatter_fusion = f32[16,128,256]{2,1,0:T(8,128)} fusion(f32[16,128,256]{2,1,0:T(8,128)} %broadcast_in_dim.50, s32[192]{0:T(256)S(1)} %copy-done.6, f32[192,128,256]{2,1,0:T(8,128)} %copy.33), kind=kCustom, calls=%fused_computation.3 | custom fusion | flops 6291456 | bytes 75498240 | tf_op jit(solution)/shard_map/scatter-add | solution.py:34
  132.4 7.2 %all-to-all-start.1 = ((f32[16,128,256]{2,1,0:T(8,128)}), f32[16,128,256]{2,1,0:T(8,128)S(1)}, u32[]{:S(2)}, u32[]{:S(2)}) async-start(f32[16,128,256]{2,1,0:T(8,128)} %scatter_fusion), calls=%async_computation.1 | async-start | bytes 4194304 | tf_op jit(solution)/shard_map/all_to_all | solution.py:36
  141.7 2.2 all_gather.9
  144.6 42.4 %all-to-all-done.1 = f32[16,128,256]{2,1,0:T(8,128)S(1)} async-done(((f32[16,128,256]{2,1,0:T(8,128)}), f32[16,128,256]{2,1,0:T(8,128)S(1)}, u32[]{:S(2)}, u32[]{:S(2)}) %all-to-all-start.1) | async-done | bytes 2097184 | tf_op jit(solution)/shard_map/all_to_all | solution.py:36
  187.0 2.0 fusion.17
  189.0 2.2 all_gather.11
  191.2 3.2 fusion.23
  194.4 10.1 %reduce-scatter.2.cloned.1.call-done = f32[512,2,256]{2,0,1:T(8,128)} async-done(((f32[512,2,512]{2,0,1:T(8,128)}), f32[512,2,256]{2,0,1:T(8,128)}) %reduce-scatter.2.cloned.1.call-update) | async-done | bytes 1048592 | tf_op jit(solution)/shard_map/reduce_scatter | solution.py:56
  207.5 7.0 %all-to-all-start.2 = ((bf16[16,128,256]{2,1,0:T(8,128)(2,1)}), bf16[16,128,256]{2,1,0:T(8,128)(2,1)S(1)}, u32[]{:S(2)}, u32[]{:S(2)}) async-start(bf16[16,128,256]{2,1,0:T(8,128)(2,1)} %broadcast_select_fusion), calls=%async_computation.3 | async-start | bytes 2097152 | tf_op jit(solution)/shard_map/all_to_all | solution.py:62
  215.3 25.0 %all-to-all-done.2 = bf16[16,128,256]{2,1,0:T(8,128)(2,1)S(1)} async-done(((bf16[16,128,256]{2,1,0:T(8,128)(2,1)}), bf16[16,128,256]{2,1,0:T(8,128)(2,1)S(1)}, u32[]{:S(2)}, u32[]{:S(2)}) %all-to-all-start.2) | async-done | bytes 1048608 | tf_op jit(solution)/shard_map/all_to_all | solution.py:62
  240.3 8.1 %gather_fusion.2 = bf16[192,128,256]{2,1,0:T(8,128)(2,1)} fusion(bf16[16,128,256]{2,1,0:T(8,128)(2,1)S(1)} %all-to-all-done.2, s32[1024]{0:T(1024)S(1)} %pad_clamp_fusion), kind=kCustom, calls=%fused_computation.2 | custom fusion | bytes 25166592 | tf_op jit(solution)/shard_map/jit(_take)/gather | solution.py:63
  248.4 16.4 %fusion.9 = f32[192,128,256]{1,2,0:T(8,128)} fusion(bf16[192,128,128]{2,1,0:T(8,128)(2,1)} %param.25, bf16[192,128,256]{2,1,0:T(8,128)(2,1)} %gather_fusion.2, pred[192]{0:T(512)(128)(4,1)S(1)} %compare_and_fusion.2), kind=kOutput, calls=%fused_computation.12 | convolution fusion | flops 1616904192 | bytes 44040384 | tf_op jit(solution)/shard_map/eij,ejc->eic/dot_general | solution.py:64
  264.8 24.7 %copy.38 = f32[192,128,256]{2,1,0:T(8,128)} copy(f32[192,128,256]{1,2,0:T(8,128)} %fusion.9) | data formatting | bytes 50331648 | tf_op jit(solution)/shard_map/eij,ejc->eic/dot_general | solution.py:64
  289.5 2.5 broadcast_in_dim.46
  291.9 56.5 %scatter_fusion.1 = f32[32,128,256]{2,1,0:T(8,128)} fusion(f32[32,128,256]{2,1,0:T(8,128)} %broadcast_in_dim.46, s32[192]{0:T(256)S(1)} %copy-done.7, f32[192,128,256]{2,1,0:T(8,128)} %copy.38), kind=kCustom, calls=%fused_computation.4 | custom fusion | flops 6291456 | bytes 75498240 | tf_op jit(solution)/shard_map/scatter-add | solution.py:67
  348.4 4.0 %fusion.14 = bf16[4096,256]{1,0:T(8,128)(2,1)} fusion(f32[32,128,256]{2,1,0:T(8,128)} %scatter_fusion.1, bf16[4096,256]{1,0:T(8,128)(2,1)S(1)} %copy-done.2), kind=kLoop, calls=%fused_computation.16 | loop fusion | flops 3145728 | bytes 8388608 | tf_op jit(solution)/shard_map/convert_element_type | solution.py:68
  (43 shorter events, 8.7 us)
Async XLA Ops:
  7.2 16.9 %copy-start = (bf16[512,256]{1,0:T(8,128)(2,1)S(1)}, bf16[512,256]{1,0:T(8,128)(2,1)}, u32[]{:S(2)}) copy-start(bf16[512,256]{1,0:T(8,128)(2,1)} %param.15) | copy-start | bytes 786436
  7.2 16.8 %all-gather.2.cloned.1.call-start = ((), (), s32[]{:S(2)}) async-start(), calls=%async_computation.4 | async-start | bytes 6291456 | tf_op jit(solution)/shard_map/all_gather | solution.py:27
  9.2 123.1 %all-to-all-start = ((s32[16,1,1]{2,1,0:T(1,128)}), s32[16,1,1]{2,1,0:T(1,128)S(1)}, u32[]{:S(2)}, u32[]{:S(2)}) async-start(s32[16,1,1]{2,1,0:T(1,128)} %copy.31), calls=%async_computation | async-start | bytes 16384 | tf_op jit(solution)/shard_map/all_to_all | solution.py:37
  52.1 26.2 %copy-start.6 = (s32[192]{0:T(256)S(1)}, s32[192]{0:T(256)}, u32[]{:S(2)}) copy-start(s32[192]{0:T(256)} %param.20) | copy-start | bytes 2308
  132.4 9.4 %copy-start.3 = (bf16[512,256]{1,0:T(8,128)(2,1)S(1)}, bf16[512,256]{1,0:T(8,128)(2,1)}, u32[]{:S(2)}) copy-start(bf16[512,256]{1,0:T(8,128)(2,1)} %param.14) | copy-start | bytes 786436
  132.4 11.5 %copy-start.5 = (bf16[512,256]{1,0:T(8,128)(2,1)S(1)}, bf16[512,256]{1,0:T(8,128)(2,1)}, u32[]{:S(2)}) copy-start(bf16[512,256]{1,0:T(8,128)(2,1)} %param.16) | copy-start | bytes 786436
  132.4 58.8 %copy-start.9 = (bf16[512,256]{1,0:T(8,128)(2,1)S(1)}, bf16[512,256]{1,0:T(8,128)(2,1)}, u32[]{:S(2)}) copy-start(bf16[512,256]{1,0:T(8,128)(2,1)} %param.17) | copy-start | bytes 786436
  132.4 54.6 %all-to-all-start.1 = ((f32[16,128,256]{2,1,0:T(8,128)}), f32[16,128,256]{2,1,0:T(8,128)S(1)}, u32[]{:S(2)}, u32[]{:S(2)}) async-start(f32[16,128,256]{2,1,0:T(8,128)} %scatter_fusion), calls=%async_computation.1 | async-start | bytes 4194304 | tf_op jit(solution)/shard_map/all_to_all | solution.py:36
  139.6 65.0 %reduce-scatter.2.cloned.1.call-start = ((), (), s32[]{:S(2)}) async-start(), calls=%async_computation.5 | async-start | bytes 3145728 | tf_op jit(solution)/shard_map/reduce_scatter | solution.py:56
  191.2 23.3 %copy-start.8 = (s32[192]{0:T(256)S(1)}, s32[192]{0:T(256)}, u32[]{:S(2)}) copy-start(s32[192]{0:T(256)} %param.23) | copy-start | bytes 2308
  204.6 9.9 %copy-start.4 = (f32[512,2,256]{2,0,1:T(8,128)S(1)}, f32[512,2,256]{2,0,1:T(8,128)}, u32[]{:S(2)}) copy-start(f32[512,2,256]{2,0,1:T(8,128)} %reduce-scatter.2.cloned.1.call-done) | copy-start | bytes 3145732
  207.5 32.8 %all-to-all-start.2 = ((bf16[16,128,256]{2,1,0:T(8,128)(2,1)}), bf16[16,128,256]{2,1,0:T(8,128)(2,1)S(1)}, u32[]{:S(2)}, u32[]{:S(2)}) async-start(bf16[16,128,256]{2,1,0:T(8,128)(2,1)} %broadcast_select_fusion), calls=%async_computation.3 | async-start | bytes 2097152 | tf_op jit(solution)/shard_map/all_to_all | solution.py:62
  264.8 27.1 %copy-start.7 = (s32[192]{0:T(256)S(1)}, s32[192]{0:T(256)}, u32[]{:S(2)}) copy-start(s32[192]{0:T(256)} %param.24) | copy-start | bytes 2308
  291.9 56.5 %copy-start.2 = (bf16[4096,256]{1,0:T(8,128)(2,1)S(1)}, bf16[4096,256]{1,0:T(8,128)(2,1)}, u32[]{:S(2)}) copy-start(bf16[4096,256]{1,0:T(8,128)(2,1)} %param.13) | copy-start | bytes 6291460
  291.9 60.4 %copy-start.1 = (bf16[512,256]{1,0:T(8,128)(2,1)S(1)}, bf16[512,256]{1,0:T(8,128)(2,1)}, u32[]{:S(2)}) copy-start(bf16[512,256]{1,0:T(8,128)(2,1)} %param.15) | copy-start | bytes 786436
Sparse Core Ops, SparseCore 0:
  9.6 14.4 all-gather.1
  194.5 9.9 reduce-scatter.1
where the time goes:
time: 361 us; the launch traced here: 359 us
  other arithmetic  118 us (33%)
  waiting for transfers between devices  84.4 us (23%)
  local copies, waits for them, and re-layouts  75 us (21%)
  matrix products  41.6 us (12%)
  starting transfers between devices  21.4 us (6%)
  between operations  14.2 us (4%)
  blocking collectives  4.35 us (1%)
    scatter-add x1, other arithmetic, per_device(): jax.ops.segment_sum(contribution, decode_target, num_segments=grid_blocks)  56.5 us
    scatter-add x1, other arithmetic, per_device(): jax.ops.segment_sum(partials, encode_slot, num_segments=band_count)  54 us
    all_to_all x1, waiting for transfers between devices, per_device(): lax.all_to_all(slot_sums, 'band', split_axis=0, concat_axis=0, tiled=True)  42.4 us
    all_to_all x1, waiting for transfers between devices, per_device(): lax.all_to_all(outgoing, 'band', split_axis=0, concat_axis=0, tiled=True)  25 us
    dot_general x1, local copies, waits for them, and re-layouts, per_device(): jnp.einsum('eij,ejc->eic', decode_tiles, picked, preferred_element_type=j...  24.7 us
    dot_general x1, local copies, waits for them, and re-layouts, per_device(): jnp.einsum('eij,ejc->eic', encode_tiles, sources, preferred_element_type=...  24.6 us
    dot_general x1, matrix products, per_device(): jnp.einsum('eij,ejc->eic', encode_tiles, sources, preferred_element_type=...  16.4 us
    dot_general x1, matrix products, per_device(): jnp.einsum('eij,ejc->eic', decode_tiles, picked, preferred_element_type=j...  16.4 us
  transfers between devices with their start and end apart: 5, of which 4 were waited for; matrix products, arithmetic and copies ran while one was open for 32% of the time, Pallas kernels for 0%

commit v1 on v0

--- a/solution.py
+++ b/solution.py
@@ -1,7 +1,104 @@
+import functools
+
 import jax
 import jax.numpy as jnp
 from jax import lax
+from jax.experimental import pallas as pl
+from jax.experimental.pallas import tpu as pltpu
 from jax.sharding import PartitionSpec as P
+
+VMEM = pltpu.VMEM
+VMEM_LIMIT = 56 * 1024 * 1024
+
+
+def divisor_at_most(count, most):
+    return max(part for part in range(1, most + 1) if count % part == 0)
+
+
+def tile_sums(group, tile_at, rows_ref, tiles_ref, into_ref, from_ref, total):
+    for local in range(group):
+        place = tile_at + local
+        product = jnp.dot(
+            tiles_ref[local], rows_ref[from_ref[place]], preferred_element_type=jnp.float32
+        )
+        total[into_ref[place]] += product
+
+
+def encode_kernel(group, source_ref, slot_ref, message_ref, tiles_ref, out_ref, total):
+    step = pl.program_id(0)
+
+    @pl.when(step == 0)
+    def _():
+        total[...] = jnp.zeros_like(total)
+
+    tile_sums(group, step * group, message_ref, tiles_ref, slot_ref, source_ref, total)
+
+    @pl.when(step == pl.num_programs(0) - 1)
+    def _():
+        out_ref[...] = total[...].astype(out_ref.dtype)
+
+
+def decode_kernel(group, slot_ref, target_ref, grid_ref, rows_ref, tiles_ref, out_ref, total):
+    step = pl.program_id(0)
+
+    @pl.when(step == 0)
+    def _():
+        total[...] = grid_ref[...].astype(jnp.float32)
+
+    tile_sums(group, step * group, rows_ref, tiles_ref, target_ref, slot_ref, total)
+
+    @pl.when(step == pl.num_programs(0) - 1)
+    def _():
+        out_ref[...] = total[...].astype(out_ref.dtype)
+
+
+def whole(array):
+    return pl.BlockSpec(array.shape, lambda step, *_: (0,) * array.ndim)
+
+
+def encode(message_blocks, tiles, source, slot, slots):
+    count, edge, _ = tiles.shape
+    width = message_blocks.shape[2]
+    group = divisor_at_most(count, 24)
+    out = jax.ShapeDtypeStruct((slots, edge, width), jnp.bfloat16)
+    return pl.pallas_call(
+        functools.partial(encode_kernel, group),
+        out_shape=out,
+        grid_spec=pltpu.PrefetchScalarGridSpec(
+            num_scalar_prefetch=2,
+            grid=(count // group,),
+            in_specs=[
+                whole(message_blocks),
+                pl.BlockSpec((group, edge, edge), lambda step, *_: (step, 0, 0)),
+            ],
+            out_specs=whole(out),
+            scratch_shapes=[VMEM((slots, edge, width), jnp.float32)],
+        ),
+        compiler_params=pltpu.CompilerParams(vmem_limit_bytes=VMEM_LIMIT),
+        name="encode",
+    )(source, slot, message_blocks, tiles)
+
+
+def decode(grid_blocks, rows, tiles, slot, target):
+    count, edge, _ = tiles.shape
+    group = divisor_at_most(count, 24)
+    return pl.pallas_call(
+        functools.partial(decode_kernel, group),
+        out_shape=jax.ShapeDtypeStruct(grid_blocks.shape, jnp.bfloat16),
+        grid_spec=pltpu.PrefetchScalarGridSpec(
+            num_scalar_prefetch=2,
+            grid=(count // group,),
+            in_specs=[
+                whole(grid_blocks),
+                whole(rows),
+                pl.BlockSpec((group, edge, edge), lambda step, *_: (step, 0, 0)),
+            ],
+            out_specs=whole(grid_blocks),
+            scratch_shapes=[VMEM(grid_blocks.shape, jnp.float32)],
+        ),
+        compiler_params=pltpu.CompilerParams(vmem_limit_bytes=VMEM_LIMIT),
+        name="decode",
+    )(slot, target, grid_blocks, rows, tiles)
 
 
 def per_device(
@@ -29,9 +126,7 @@
         jnp.dot(full_grid, send_weight, preferred_element_type=jnp.float32)
     ).astype(jnp.bfloat16)
     message_blocks = message.reshape(grid_blocks, tile_edge, feature_width)
-    sources = jnp.take(message_blocks, encode_source, axis=0)
-    partials = jnp.einsum("eij,ejc->eic", encode_tiles, sources, preferred_element_type=jnp.float32)
-    slot_sums = jax.ops.segment_sum(partials, encode_slot, num_segments=band_count)
+    slot_sums = encode(message_blocks, encode_tiles, encode_source, encode_slot, band_count)
     arrived, owner_block = (
         lax.all_to_all(slot_sums, "band", split_axis=0, concat_axis=0, tiled=True),
         lax.all_to_all(slot_block[0], "band", split_axis=0, concat_axis=0, tiled=True),
@@ -39,7 +134,7 @@
     selector = (owner_block[None, :] == jnp.arange(mesh_blocks, dtype=jnp.int32)[:, None]).astype(
         jnp.float32
     )
-    aggregate = jnp.einsum("bs,sic->bic", selector, arrived, precision=lax.Precision.HIGHEST)
+    aggregate = jnp.einsum("bs,sic->bic", selector, arrived.astype(jnp.float32), precision=lax.Precision.HIGHEST)
     pooled = aggregate.reshape(-1, feature_width).astype(jnp.bfloat16)
     mesh_full, pooled_full = (
         lax.all_gather(mesh_nodes, "mp", axis=1, tiled=True),
@@ -58,16 +153,18 @@
     decode_source = (
         reduced[:, 1, :].astype(jnp.bfloat16).reshape(mesh_blocks, tile_edge, feature_width)
     )
-    outgoing = jnp.take(decode_source, owner_block, axis=0)
+    outgoing = sum(
+        jnp.where(owner_block[:, None, None] == block, decode_source[block], 0)
+        for block in range(mesh_blocks)
+    )
     returned = lax.all_to_all(outgoing, "band", split_axis=0, concat_axis=0, tiled=True)
-    picked = jnp.take(returned, decode_slot, axis=0)
-    contribution = jnp.einsum(
-        "eij,ejc->eic", decode_tiles, picked, preferred_element_type=jnp.float32
-    )
-    grid_sum = jax.ops.segment_sum(contribution, decode_target, num_segments=grid_blocks)
-    grid_state = (grid_nodes.astype(jnp.float32) + grid_sum.reshape(-1, feature_width)).astype(
-        jnp.bfloat16
-    )
+    grid_state = decode(
+        grid_nodes.reshape(grid_blocks, tile_edge, feature_width),
+        returned,
+        decode_tiles,
+        decode_slot,
+        decode_target,
+    ).reshape(grid_nodes.shape)
     return (grid_state, mesh_state)
 
 

time: 361 us -> 142 us (0.39)
  other arithmetic: 118 us -> 5.21 us
  local copies, waits for them, and re-layouts: 75 us -> 2.64 us
  matrix products: 41.6 us -> 7.87 us
  Pallas kernels: 0 us -> 21.5 us
  waiting for transfers between devices: 84.4 us -> 64 us
    scatter-add x2 -> x0, other arithmetic: 111 us -> none  [the longest x1 56.5 us: per_device(): jax.ops.segment_sum(contribution, decode_target, num_segments=grid_blocks)]
    dot_general x2 -> x0, local copies, waits for them, and re-layouts: 49.3 us -> none  [the longest x1 24.7 us: per_device(): jnp.einsum('eij,ejc->eic', decode_tiles, picked, preferred_element_type=j...]
    dot_general x3 -> x1, matrix products: 34.7 us -> 0.67 us  [per_device(): jnp.einsum('bs,sic->bic', selector, arrived.astype(jnp.float32), precisio...]
    pallas_call x0 -> x2, Pallas kernels: none -> 21.5 us  [the longest x1 11.1 us: decode(): pl.pallas_call(functools.partial(decode_kernel, group), out_shape=jax.Sha...]
    all_to_all x1, waiting for transfers between devices: 42.4 us -> 22.6 us  [per_device(): lax.all_to_all(slot_sums, 'band', split_axis=0, concat_axis=0, tiled=True)]
    gather x3 -> x0, local copies, waits for them, and re-layouts: 17 us -> none  [the longest x1 8.29 us: per_device(): sources = jnp.take(message_blocks, encode_source, axis=0)]
    broadcast_in_dim x2 -> x0, local copies, waits for them, and re-layouts: 3.99 us -> none  [the longest x1 2.46 us: per_device(): jax.ops.segment_sum(contribution, decode_target, num_segments=grid_blocks)]
    convert_element_type x1 -> x0, other arithmetic: 3.97 us -> none  [per_device(): (grid_nodes.astype(jnp.float32) + grid_sum.reshape(-1, feature_width)).as...]
  transfers between devices with their start and end apart: 5 -> 5, of which waited for: 4 -> 4; matrix products, arithmetic and copies ran while one was open for 32% -> 6% of each run, Pallas kernels for 0% -> 7%
where the time goes in v1:
time: 142 us; the launch traced here: 141 us
  waiting for transfers between devices  64 us (45%)
  Pallas kernels  21.5 us (15%)
  starting transfers between devices  21.4 us (15%)
  between operations  14.1 us (10%)
  matrix products  7.87 us (6%)
  other arithmetic  5.21 us (4%)
  blocking collectives  4.36 us (3%)
  local copies, waits for them, and re-layouts  2.64 us (2%)
    all_to_all x1, waiting for transfers between devices, per_device(): lax.all_to_all(outgoing, 'band', split_axis=0, concat_axis=0, tiled=True)  25.1 us
    all_to_all x1, waiting for transfers between devices, per_device(): lax.all_to_all(slot_sums, 'band', split_axis=0, concat_axis=0, tiled=True)  22.6 us
    pallas_call x1, Pallas kernels, decode(): pl.pallas_call(functools.partial(decode_kernel, group), out_shape=jax.Sha...  11.1 us
    pallas_call x1, Pallas kernels, encode(): pl.pallas_call(functools.partial(encode_kernel, group), out_shape=out, gr...  10.4 us
    reduce_scatter x1, waiting for transfers between devices, per_device(): lax.psum_scatter(partial_out, 'mp', scatter_dimension=2, tiled=True)  8.02 us
    all_gather x1, waiting for transfers between devices, per_device(): full_grid = lax.all_gather(grid_nodes, 'mp', axis=1, tiled=True)  7.55 us
    all_to_all x1, starting transfers between devices, per_device(): lax.all_to_all(slot_block[0], 'band', split_axis=0, concat_axis=0, tiled=...  7.22 us
    all_to_all x1, starting transfers between devices, per_device(): lax.all_to_all(slot_sums, 'band', split_axis=0, concat_axis=0, tiled=True)  7.12 us
  transfers between devices with their start and end apart: 5, of which 4 were waited for; matrix products, arithmetic and copies ran while one was open for 6% of the time, Pallas kernels for 7%

profile of v1, /device:TPU:8, one launch (start us, length us, event | category | flops | bytes accessed | tf_op | source)
XLA Modules:
  0.0 141.1 jit_solution(12632821104813302964)
XLA Ops:
  7.2 0.7 all-gather.2.cloned.1.call-update
  7.9 1.3 copy.24
  9.2 7.2 %all-to-all-start = ((s32[16,1,1]{2,1,0:T(1,128)}), s32[16,1,1]{2,1,0:T(1,128)S(1)}, u32[]{:S(2)}, u32[]{:S(2)}) async-start(s32[16,1,1]{2,1,0:T(1,128)} %copy.24), calls=%async_computation | async-start | bytes 16384 | tf_op jit(solution)/shard_map/all_to_all | solution.py:132
  16.5 7.5 %all-gather.2.cloned.1.call-done = bf16[4096,512]{1,0:T(8,128)(2,1)} async-done(((bf16[4096,256]{1,0:T(8,128)(2,1)}), bf16[4096,512]{1,0:T(8,128)(2,1)}) %all-gather.2.cloned.1.call-update) | async-done | bytes 4194320 | tf_op jit(solution)/shard_map/all_gather | solution.py:124
  24.0 4.8 %multiply_convert_fusion = bf16[4096,256]{1,0:T(8,128)(2,1)} fusion(bf16[4096,512]{1,0:T(8,128)(2,1)} %all-gather.2.cloned.1.call-done, bf16[512,256]{1,0:T(8,128)(2,1)S(1)} %copy-done), kind=kOutput, calls=%fused_computation | convolution fusion | flops 1078984704 | bytes 6553600 | tf_op jit(solution)/shard_map/dot_general | solution.py:126
  28.8 10.4 %encode.1 = bf16[16,128,256]{2,1,0:T(8,128)(2,1)} custom-call(s32[192]{0:T(256)} %source_ref.1, s32[192]{0:T(256)} %slot_ref.2, bf16[32,128,256]{2,1,0:T(8,128)(2,1)} %bitcast.39, bf16[192,128,128]{2,1,0:T(8,128)(2,1)} %tiles_ref.2), custom_call_target="tpu_custom_call" | custom-call | tf_op jit(solution)/shard_map/encode/pallas_call | solution.py:64
  39.2 7.1 %all-to-all-start.1 = ((bf16[16,128,256]{2,1,0:T(8,128)(2,1)}), bf16[16,128,256]{2,1,0:T(8,128)(2,1)S(1)}, u32[]{:S(2)}, u32[]{:S(2)}) async-start(bf16[16,128,256]{2,1,0:T(8,128)(2,1)} %encode.1), calls=%async_computation.1 | async-start | bytes 2097152 | tf_op jit(solution)/shard_map/all_to_all | solution.py:131
  46.4 0.2 copy.27
  46.7 2.2 %all_gather.9 = bf16[512,512]{1,0:T(8,128)(2,1)S(1)} all-gather(bf16[512,256]{1,0:T(8,128)(2,1)S(1)} %copy-done.3), channel_id=1, replica_groups=mesh['band'=16,'mp'=2] {'mp'}, dimensions={1}, use_global_device_ids=true | all-gather | bytes 786432 | tf_op jit(solution)/shard_map/all_gather | solution.py:140
  48.9 0.3 fusion.10
  49.2 0.4 reduce.1
  49.5 22.6 %all-to-all-done.1 = bf16[16,128,256]{2,1,0:T(8,128)(2,1)S(1)} async-done(((bf16[16,128,256]{2,1,0:T(8,128)(2,1)}), bf16[16,128,256]{2,1,0:T(8,128)(2,1)S(1)}, u32[]{:S(2)}, u32[]{:S(2)}) %all-to-all-start.1) | async-done | bytes 1048608 | tf_op jit(solution)/shard_map/all_to_all | solution.py:131
  72.2 0.7 convolution_convert_fusion
  72.9 2.2 %all_gather.11 = bf16[512,512]{1,0:T(8,128)(2,1)S(1)} all-gather(bf16[512,256]{1,0:T(8,128)(2,1)S(1)} %bitcast.42), channel_id=1, replica_groups=mesh['band'=16,'mp'=2] {'mp'}, dimensions={1}, use_global_device_ids=true | all-gather | bytes 786432 | tf_op jit(solution)/shard_map/all_gather | solution.py:141
  75.1 2.1 %fusion.4 = f32[512,2,512]{2,0,1:T(8,128)} fusion(bf16[2,512,256]{2,1,0:T(8,128)(2,1)S(1)} %bitcast.44, f32[512,256]{1,0:T(8,128)S(1)} %fusion.10, bf16[512,512]{1,0:T(8,128)(2,1)S(1)} %all_gather.11, bf16[512,256]{1,0:T(8,128)(2,1)S(1)} %copy-done.6), kind=kOutput, calls=%fused_computation.10 | convolution fusion | flops 403439616 | bytes 3932160 | tf_op jit(solution)/shard_map/dot_general | solution.py:147
  77.2 1.2 compare_reduce_fusion.3
  78.5 8.0 %reduce-scatter.2.cloned.1.call-done = f32[512,2,256]{2,0,1:T(8,128)} async-done(((f32[512,2,512]{2,0,1:T(8,128)}), f32[512,2,256]{2,0,1:T(8,128)}) %reduce-scatter.2.cloned.1.call-update) | async-done | bytes 1048592 | tf_op jit(solution)/shard_map/reduce_scatter | solution.py:151
  86.5 1.4 convert.3
  87.9 1.5 %select_add_fusion = bf16[16,128,256]{2,1,0:T(8,128)(2,1)} fusion(pred[16]{0:T(512)(128)(4,1)S(1)} %get-tuple-element.3, pred[16]{0:T(512)(128)(4,1)S(1)} %get-tuple-element.4, pred[16]{0:T(512)(128)(4,1)S(1)} %get-tuple-element.5, pred[16]{0:T(512)(128)(4,1)S(1)} %get-tuple-element.2, bf16[128,256]{1,0:T(8,128)(2,1)S(1)} %get-tuple-element.7, ...), kind=kLoop, calls=%fused_computation.4 | loop fusion | flops 3670016 | bytes 1310784 | tf_op jit(solution)/shard_map/add | solution.py:156
  89.3 7.0 %all-to-all-start.2 = ((bf16[16,128,256]{2,1,0:T(8,128)(2,1)}), bf16[16,128,256]{2,1,0:T(8,128)(2,1)S(1)}, u32[]{:S(2)}, u32[]{:S(2)}) async-start(bf16[16,128,256]{2,1,0:T(8,128)(2,1)} %select_add_fusion), calls=%async_computation.3 | async-start | bytes 2097152 | tf_op jit(solution)/shard_map/all_to_all | solution.py:160
  96.3 0.8 fusion.2
  97.1 25.1 %all-to-all-done.2.rows_ref = bf16[16,128,256]{2,1,0:T(8,128)(2,1)S(1)} async-done(((bf16[16,128,256]{2,1,0:T(8,128)(2,1)}), bf16[16,128,256]{2,1,0:T(8,128)(2,1)S(1)}, u32[]{:S(2)}, u32[]{:S(2)}) %all-to-all-start.2) | async-done | bytes 1048608 | tf_op jit(solution)/shard_map/all_to_all | solution.py:160
  122.2 1.0 copy-done.1
  123.1 11.1 %decode.1 = bf16[32,128,256]{2,1,0:T(8,128)(2,1)} custom-call(s32[192]{0:T(256)} %slot_ref.3, s32[192]{0:T(256)} %target_ref.1, bf16[32,128,256]{2,1,0:T(8,128)(2,1)} %bitcast.38, bf16[16,128,256]{2,1,0:T(8,128)(2,1)} %copy-done.1, bf16[192,128,128]{2,1,0:T(8,128)(2,1)} %tiles_ref.3), custom_call_target="tpu_custom_call" | custom-call | tf_op jit(solution)/shard_map/decode/pallas_call | solution.py:85
  (20 shorter events, 0.2 us)
Async XLA Ops:
  7.2 16.9 %copy-start = (bf16[512,256]{1,0:T(8,128)(2,1)S(1)}, bf16[512,256]{1,0:T(8,128)(2,1)}, u32[]{:S(2)}) copy-start(bf16[512,256]{1,0:T(8,128)(2,1)} %param.15) | copy-start | bytes 786436
  7.2 16.8 %all-gather.2.cloned.1.call-start = ((), (), s32[]{:S(2)}) async-start(), calls=%async_computation.4 | async-start | bytes 6291456 | tf_op jit(solution)/shard_map/all_gather | solution.py:124
  9.2 30.0 %all-to-all-start = ((s32[16,1,1]{2,1,0:T(1,128)}), s32[16,1,1]{2,1,0:T(1,128)S(1)}, u32[]{:S(2)}, u32[]{:S(2)}) async-start(s32[16,1,1]{2,1,0:T(1,128)} %copy.24), calls=%async_computation | async-start | bytes 16384 | tf_op jit(solution)/shard_map/all_to_all | solution.py:132
  28.8 17.6 %copy-start.4 = (bf16[256,2,512]{2,1,0:T(2,128)(2,1)S(1)}, bf16[256,2,512]{2,1,0:T(2,128)(2,1)}, u32[]{:S(2)}) copy-start(bf16[256,2,512]{2,1,0:T(2,128)(2,1)} %param.18) | copy-start | bytes 1572868
  39.2 7.5 %copy-start.3 = (bf16[512,256]{1,0:T(8,128)(2,1)S(1)}, bf16[512,256]{1,0:T(8,128)(2,1)}, u32[]{:S(2)}) copy-start(bf16[512,256]{1,0:T(8,128)(2,1)} %param.14) | copy-start | bytes 786436
  39.2 9.7 %copy-start.5 = (bf16[512,256]{1,0:T(8,128)(2,1)S(1)}, bf16[512,256]{1,0:T(8,128)(2,1)}, u32[]{:S(2)}) copy-start(bf16[512,256]{1,0:T(8,128)(2,1)} %param.16) | copy-start | bytes 786436
  39.2 35.9 %copy-start.6 = (bf16[512,256]{1,0:T(8,128)(2,1)S(1)}, bf16[512,256]{1,0:T(8,128)(2,1)}, u32[]{:S(2)}) copy-start(bf16[512,256]{1,0:T(8,128)(2,1)} %param.17) | copy-start | bytes 786436
  39.2 33.0 %all-to-all-start.1 = ((bf16[16,128,256]{2,1,0:T(8,128)(2,1)}), bf16[16,128,256]{2,1,0:T(8,128)(2,1)S(1)}, u32[]{:S(2)}, u32[]{:S(2)}) async-start(bf16[16,128,256]{2,1,0:T(8,128)(2,1)} %encode.1), calls=%async_computation.1 | async-start | bytes 2097152 | tf_op jit(solution)/shard_map/all_to_all | solution.py:131
  46.3 40.2 %reduce-scatter.2.cloned.1.call-start = ((), (), s32[]{:S(2)}) async-start(), calls=%async_computation.5 | async-start | bytes 3145728 | tf_op jit(solution)/shard_map/reduce_scatter | solution.py:151
  86.5 9.8 %copy-start.2 = (f32[512,2,256]{2,0,1:T(8,128)S(1)}, f32[512,2,256]{2,0,1:T(8,128)}, u32[]{:S(2)}) copy-start(f32[512,2,256]{2,0,1:T(8,128)} %reduce-scatter.2.cloned.1.call-done) | copy-start | bytes 3145732
  89.3 32.8 %all-to-all-start.2 = ((bf16[16,128,256]{2,1,0:T(8,128)(2,1)}), bf16[16,128,256]{2,1,0:T(8,128)(2,1)S(1)}, u32[]{:S(2)}, u32[]{:S(2)}) async-start(bf16[16,128,256]{2,1,0:T(8,128)(2,1)} %select_add_fusion), calls=%async_computation.3 | async-start | bytes 2097152 | tf_op jit(solution)/shard_map/all_to_all | solution.py:160
  122.2 1.0 copy-start.1
Sparse Core Ops, SparseCore 0:
  9.5 14.4 all-gather.1
  77.3 9.1 reduce-scatter.1

commit v2 on v1

--- a/solution.py
+++ b/solution.py
@@ -99,6 +99,278 @@
         compiler_params=pltpu.CompilerParams(vmem_limit_bytes=VMEM_LIMIT),
         name="decode",
     )(slot, target, grid_blocks, rows, tiles)
+
+
+def silu(value):
+    return value / (1.0 + jnp.exp(-value))
+
+
+def push(source, target, send_sem, recv_sem, device):
+    return pltpu.make_async_remote_copy(
+        src_ref=source,
+        dst_ref=target,
+        send_sem=send_sem,
+        recv_sem=recv_sem,
+        device_id=device,
+        device_id_type=pl.DeviceIdType.MESH,
+    )
+
+
+def matmul(left, right):
+    return jnp.dot(left, right, preferred_element_type=jnp.float32)
+
+
+def message_kernel(parts, grid_hbm, weight_ref, out_ref, own, other, load_sem, send_sem, recv_sem):
+    me = lax.axis_index("mp")
+    peer = 1 - me
+    rows = own.shape[0] // parts
+    half = own.shape[1]
+
+    def part(ref, at):
+        return ref.at[pl.ds(at * rows, rows)]
+
+    loads = [
+        pltpu.make_async_copy(part(grid_hbm, at), part(own, at), load_sem.at[at])
+        for at in range(parts)
+    ]
+    for load in loads:
+        load.start()
+    barrier = pltpu.get_barrier_semaphore()
+    pl.semaphore_signal(
+        barrier, inc=1, device_id={"mp": peer}, device_id_type=pl.DeviceIdType.MESH
+    )
+    pl.semaphore_wait(barrier, 1)
+    sends = [
+        push(part(grid_hbm, at), part(other, at), send_sem.at[at], recv_sem.at[at], {"mp": peer})
+        for at in range(parts)
+    ]
+    for send in sends:
+        send.start()
+    own_weight = weight_ref[pl.ds(pl.multiple_of(me * half, half), half), :]
+    other_weight = weight_ref[pl.ds(pl.multiple_of(peer * half, half), half), :]
+    for at in range(parts):
+        loads[at].wait()
+        sends[at].wait_recv()
+        span = pl.ds(at * rows, rows)
+        total = matmul(own[span, :], own_weight) + matmul(other[span, :], other_weight)
+        out_ref[span, :] = silu(total).astype(out_ref.dtype)
+    for send in sends:
+        send.wait_send()
+
+
+def messages(grid_nodes, send_weight):
+    rows, half = grid_nodes.shape
+    parts = 8
+    return pl.pallas_call(
+        functools.partial(message_kernel, parts),
+        out_shape=jax.ShapeDtypeStruct((rows, send_weight.shape[1]), jnp.bfloat16),
+        in_specs=[pl.BlockSpec(memory_space=pl.ANY), pl.BlockSpec(memory_space=VMEM)],
+        out_specs=pl.BlockSpec(memory_space=VMEM),
+        scratch_shapes=[VMEM((rows, half), jnp.bfloat16)] * 2
+        + [pltpu.SemaphoreType.DMA((parts,))] * 3,
+        compiler_params=pltpu.CompilerParams(
+            collective_id=0, has_side_effects=True, vmem_limit_bytes=VMEM_LIMIT
+        ),
+        name="messages",
+    )(grid_nodes, send_weight)
+
+
+def node_kernel(
+    sums_ref, linked_ref, mesh_ref, self_ref, pooled_weight_ref, out_weight_ref,
+    state_ref, returned_ref,
+    link_out, link_in, arrived, mesh_other, weight_other, pooled, pooled_other,
+    hidden, hidden_other, inner, total, projected, stage,
+    link_send, link_recv, sum_send, sum_recv, back_send, back_recv, mp_send, mp_recv,
+):
+    bands = sums_ref.shape[0]
+    blocks, edge, half = total.shape
+    width = self_ref.shape[1] * 2
+    me = lax.axis_index("band")
+    core = lax.axis_index("mp")
+    peer = 1 - core
+    across = {"mp": peer}
+    mine = pl.multiple_of(core * half, half)
+    theirs = pl.multiple_of(peer * half, half)
+
+    barrier = pltpu.get_barrier_semaphore()
+
+    def greet(hop, carry):
+        pl.semaphore_signal(
+            barrier,
+            inc=1,
+            device_id={"band": lax.rem(me + hop, bands)},
+            device_id_type=pl.DeviceIdType.MESH,
+        )
+        return carry
+
+    lax.fori_loop(1, bands, greet, 0)
+    pl.semaphore_signal(barrier, inc=1, device_id=across, device_id_type=pl.DeviceIdType.MESH)
+
+    def spread(patch, carry):
+        link_out[patch] = jnp.full(link_out.shape[1:], linked_ref[0, patch], jnp.int32)
+        return carry
+
+    lax.fori_loop(0, bands, spread, 0)
+    pl.semaphore_wait(barrier, bands)
+
+    def link_copy(patch):
+        return push(
+            link_out.at[patch], link_in.at[me], link_send.at[patch], link_recv.at[me],
+            {"band": patch},
+        )
+
+    def sum_copy(patch):
+        return push(
+            sums_ref.at[patch], arrived.at[me], sum_send.at[patch], sum_recv.at[me],
+            {"band": patch},
+        )
+
+    def back_copy(band):
+        return push(
+            stage.at[band], returned_ref.at[me], back_send.at[band], back_recv.at[me],
+            {"band": band},
+        )
+
+    def send_links(hop, carry):
+        link_copy(lax.rem(me + hop, bands)).start()
+        return carry
+
+    def send_sums(hop, carry):
+        sum_copy(lax.rem(me + hop, bands)).start()
+        return carry
+
+    lax.fori_loop(1, bands, send_links, 0)
+    lax.fori_loop(1, bands, send_sums, 0)
+
+    mesh_copy = push(mesh_ref, mesh_other, mp_send.at[0], mp_recv.at[0], across)
+    mesh_copy.start()
+    weight_copies = [
+        push(
+            out_weight_ref.at[:, pl.ds(pl.multiple_of(which * width + theirs, half), half)],
+            weight_other.at[which],
+            mp_send.at[1 + which],
+            mp_recv.at[1 + which],
+            across,
+        )
+        for which in range(2)
+    ]
+    for copy in weight_copies:
+        copy.start()
+
+    inner[...] = matmul(mesh_ref[...], self_ref[pl.ds(mine, half), :])
+    mesh_copy.wait()
+    inner[...] += matmul(mesh_other[...], self_ref[pl.ds(theirs, half), :])
+
+    own = sums_ref[me].astype(jnp.float32)
+    own_link = link_out[me, 0:1, :]
+    for block in range(blocks):
+        total[block] = jnp.where(own_link == block, own, 0.0)
+
+    def gather(hop, carry):
+        band = lax.rem(me + bands - hop, bands)
+        push(
+            link_out.at[band], link_in.at[band], link_send.at[band], link_recv.at[band],
+            {"band": band},
+        ).wait_recv()
+        push(
+            sums_ref.at[band], arrived.at[band], sum_send.at[band], sum_recv.at[band],
+            {"band": band},
+        ).wait_recv()
+        value = arrived[band].astype(jnp.float32)
+        link = link_in[band, 0:1, :]
+        for block in range(blocks):
+            total[block] += jnp.where(link == block, value, 0.0)
+        return carry
+
+    lax.fori_loop(1, bands, gather, 0)
+
+    pooled[...] = total[...].reshape(pooled.shape).astype(pooled.dtype)
+    pooled_copy = push(pooled, pooled_other, mp_send.at[3], mp_recv.at[3], across)
+    pooled_copy.start()
+    inner[...] += matmul(pooled[...], pooled_weight_ref[pl.ds(mine, half), :])
+    pooled_copy.wait()
+    inner[...] += matmul(pooled_other[...], pooled_weight_ref[pl.ds(theirs, half), :])
+    hidden[...] = silu(inner[...]).astype(hidden.dtype)
+    hidden_copy = push(hidden, hidden_other, mp_send.at[4], mp_recv.at[4], across)
+    hidden_copy.start()
+    for which in range(2):
+        columns = pl.ds(pl.multiple_of(which * width + mine, half), half)
+        projected[which] = matmul(hidden[...], out_weight_ref[:, columns])
+    for copy in weight_copies:
+        copy.wait()
+    hidden_copy.wait()
+    source = projected[1] + matmul(hidden_other[...], weight_other[1])
+    total[...] = source.astype(jnp.bfloat16).astype(jnp.float32).reshape(total.shape)
+
+    def picked(link):
+        value = total[0]
+        for block in range(1, blocks):
+            value = jnp.where(link == block, total[block], value)
+        return value.astype(stage.dtype)
+
+    def send_back(hop, carry):
+        band = lax.rem(me + hop, bands)
+        stage[band] = picked(link_in[band, 0:1, :])
+        back_copy(band).start()
+        return carry
+
+    lax.fori_loop(1, bands, send_back, 0)
+    returned_ref[me] = picked(own_link)
+    residual = projected[0] + matmul(hidden_other[...], weight_other[0])
+    state_ref[...] = (mesh_ref[...].astype(jnp.float32) + residual).astype(state_ref.dtype)
+
+    def finish(hop, carry):
+        band = lax.rem(me + bands - hop, bands)
+        push(
+            stage.at[band], returned_ref.at[band], back_send.at[band], back_recv.at[band],
+            {"band": band},
+        ).wait_recv()
+        link_copy(band).wait_send()
+        sum_copy(band).wait_send()
+        back_copy(band).wait_send()
+        return carry
+
+    lax.fori_loop(1, bands, finish, 0)
+
+
+def update_nodes(sums, linked, mesh_nodes, self_weight, pooled_weight, out_weight):
+    bands, edge, half = sums.shape
+    rows = mesh_nodes.shape[0]
+    flat_weight = out_weight.reshape(out_weight.shape[0], -1)
+    nodes = VMEM((rows, half), jnp.bfloat16)
+    by_band = pltpu.SemaphoreType.DMA((bands,))
+    by_use = pltpu.SemaphoreType.DMA((5,))
+    vmem = pl.BlockSpec(memory_space=VMEM)
+    return pl.pallas_call(
+        node_kernel,
+        out_shape=(
+            jax.ShapeDtypeStruct(mesh_nodes.shape, jnp.bfloat16),
+            jax.ShapeDtypeStruct(sums.shape, jnp.bfloat16),
+        ),
+        in_specs=[vmem, pl.BlockSpec(memory_space=pltpu.SMEM)] + [vmem] * 4,
+        out_specs=(vmem, vmem),
+        scratch_shapes=[
+            VMEM((bands, 8, half), jnp.int32),
+            VMEM((bands, 8, half), jnp.int32),
+            VMEM(sums.shape, jnp.bfloat16),
+            nodes,
+            VMEM((2, out_weight.shape[0], half), jnp.bfloat16),
+            nodes,
+            nodes,
+            nodes,
+            nodes,
+            VMEM((rows, half), jnp.float32),
+            VMEM((rows // edge, edge, half), jnp.float32),
+            VMEM((2, rows, half), jnp.float32),
+            VMEM(sums.shape, jnp.bfloat16),
+        ]
+        + [by_band] * 6
+        + [by_use] * 2,
+        compiler_params=pltpu.CompilerParams(
+            collective_id=1, has_side_effects=True, vmem_limit_bytes=VMEM_LIMIT
+        ),
+        name="update_nodes",
+    )(sums, linked, mesh_nodes, self_weight, pooled_weight, flat_weight)
 
 
 def per_device(
@@ -120,44 +392,12 @@
     tile_edge = encode_tiles.shape[1]
     feature_width = grid_nodes.shape[1]
     grid_blocks = grid_nodes.shape[0] // tile_edge
-    mesh_blocks = mesh_nodes.shape[0] // tile_edge
-    full_grid = lax.all_gather(grid_nodes, "mp", axis=1, tiled=True)
-    message = jax.nn.silu(
-        jnp.dot(full_grid, send_weight, preferred_element_type=jnp.float32)
-    ).astype(jnp.bfloat16)
+    message = messages(grid_nodes, send_weight)
     message_blocks = message.reshape(grid_blocks, tile_edge, feature_width)
     slot_sums = encode(message_blocks, encode_tiles, encode_source, encode_slot, band_count)
-    arrived, owner_block = (
-        lax.all_to_all(slot_sums, "band", split_axis=0, concat_axis=0, tiled=True),
-        lax.all_to_all(slot_block[0], "band", split_axis=0, concat_axis=0, tiled=True),
+    mesh_state, returned = update_nodes(
+        slot_sums, slot_block, mesh_nodes, self_weight, pooled_weight, out_weight
     )
-    selector = (owner_block[None, :] == jnp.arange(mesh_blocks, dtype=jnp.int32)[:, None]).astype(
-        jnp.float32
-    )
-    aggregate = jnp.einsum("bs,sic->bic", selector, arrived.astype(jnp.float32), precision=lax.Precision.HIGHEST)
-    pooled = aggregate.reshape(-1, feature_width).astype(jnp.bfloat16)
-    mesh_full, pooled_full = (
-        lax.all_gather(mesh_nodes, "mp", axis=1, tiled=True),
-        lax.all_gather(pooled, "mp", axis=1, tiled=True),
-    )
-    inner_sum = jnp.dot(mesh_full, self_weight, preferred_element_type=jnp.float32) + jnp.dot(
-        pooled_full, pooled_weight, preferred_element_type=jnp.float32
-    )
-    hidden = jax.nn.silu(inner_sum).astype(jnp.bfloat16)
-    partial_out = jnp.dot(
-        hidden, out_weight.reshape(hidden.shape[1], -1), preferred_element_type=jnp.float32
-    )
-    partial_out = partial_out.reshape(hidden.shape[0], 2, -1)
-    reduced = lax.psum_scatter(partial_out, "mp", scatter_dimension=2, tiled=True)
-    mesh_state = (mesh_nodes.astype(jnp.float32) + reduced[:, 0, :]).astype(jnp.bfloat16)
-    decode_source = (
-        reduced[:, 1, :].astype(jnp.bfloat16).reshape(mesh_blocks, tile_edge, feature_width)
-    )
-    outgoing = sum(
-        jnp.where(owner_block[:, None, None] == block, decode_source[block], 0)
-        for block in range(mesh_blocks)
-    )
-    returned = lax.all_to_all(outgoing, "band", split_axis=0, concat_axis=0, tiled=True)
     grid_state = decode(
         grid_nodes.reshape(grid_blocks, tile_edge, feature_width),
         returned,

time: 142 us -> 95.2 us (0.67)
  the two profiles are of different devices: /device:TPU:8 before, /device:TPU:30 now
where the time goes in v2:
time: 95.2 us; the launch traced here: 94.8 us
  Pallas kernels  92.5 us (97%)
  local copies, waits for them, and re-layouts  1.59 us (2%)
    pallas_call x1, Pallas kernels, update_nodes(): pl.pallas_call(node_kernel, out_shape=(jax.ShapeDtypeStruct(mesh_nodes.sh...  63 us
    pallas_call x1, Pallas kernels, decode(): pl.pallas_call(functools.partial(decode_kernel, group), out_shape=jax.Sha...  11.3 us
    pallas_call x1, Pallas kernels, encode(): pl.pallas_call(functools.partial(encode_kernel, group), out_shape=out, gr...  10.4 us
    pallas_call x1, Pallas kernels, messages(): pl.pallas_call(functools.partial(message_kernel, parts), out_shape=jax.Sh...  7.79 us

profile of v2, /device:TPU:30, one launch (start us, length us, event | category | flops | bytes accessed | tf_op | source)
XLA Modules:
  0.0 94.8 jit_solution(5307330059159268622)
XLA Ops:
  0.6 7.8 %messages.1 = bf16[4096,256]{1,0:T(8,128)(2,1)} custom-call(bf16[4096,256]{1,0:T(8,128)(2,1)} %grid_hbm.1, bf16[512,256]{1,0:T(8,128)(2,1)} %weight_ref.1), custom_call_target="tpu_custom_call" | custom-call | tf_op jit(solution)/shard_map/messages/pallas_call | solution.py:164
  8.4 0.0 copy-start
  8.4 10.4 %encode.1.sums_ref = bf16[16,128,256]{2,1,0:T(8,128)(2,1)} custom-call(s32[192]{0:T(256)} %source_ref.1, s32[192]{0:T(256)} %slot_ref.2, bf16[32,128,256]{2,1,0:T(8,128)(2,1)} %bitcast.5, bf16[192,128,128]{2,1,0:T(8,128)(2,1)} %tiles_ref.2), custom_call_target="tpu_custom_call" | custom-call | tf_op jit(solution)/shard_map/encode/pallas_call | solution.py:64
  18.8 0.0 copy-done
  18.8 0.9 copy.15
  19.7 63.0 %update_nodes.1 = (bf16[512,256]{1,0:T(8,128)(2,1)}, bf16[16,128,256]{2,1,0:T(8,128)(2,1)}) custom-call(bf16[16,128,256]{2,1,0:T(8,128)(2,1)} %encode.1.sums_ref, s32[1,16]{1,0:T(1,128)} %linked_ref.1, bf16[512,256]{1,0:T(8,128)(2,1)} %mesh_ref.1, bf16[512,256]{1,0:T(8,128)(2,1)} %self_ref.1, bf16[512,256]{1,0:T(8,128)(2,1)} %pooled_weight_ref.1, ...), custom_call_target="tpu_custom_call" | custom-call | tf_op jit(solution)/shard_map/update_nodes/pallas_call | solution.py:344
  82.8 0.0 copy-start.1
  82.8 11.3 %decode.1 = bf16[32,128,256]{2,1,0:T(8,128)(2,1)} custom-call(s32[192]{0:T(256)} %slot_ref.3, s32[192]{0:T(256)} %target_ref.1, bf16[32,128,256]{2,1,0:T(8,128)(2,1)} %bitcast.6, bf16[16,128,256]{2,1,0:T(8,128)(2,1)} %get-tuple-element.4.rows_ref, bf16[192,128,128]{2,1,0:T(8,128)(2,1)} %tiles_ref.3), custom_call_target="tpu_custom_call" | custom-call | tf_op jit(solution)/shard_map/decode/pallas_call | solution.py:85
  94.1 0.0 copy-done.1
  94.1 0.7 copy.17
Async XLA Ops:
  8.4 10.4 %copy-start = (bf16[256,2,512]{2,1,0:T(2,128)(2,1)S(1)}, bf16[256,2,512]{2,1,0:T(2,128)(2,1)}, u32[]{:S(2)}) copy-start(bf16[256,2,512]{2,1,0:T(2,128)(2,1)} %param.18) | copy-start | bytes 1572868
  82.8 11.3 %copy-start.1 = (bf16[512,256]{1,0:T(8,128)(2,1)S(1)}, bf16[512,256]{1,0:T(8,128)(2,1)}, u32[]{:S(2)}) copy-start(bf16[512,256]{1,0:T(8,128)(2,1)} %get-tuple-element.9) | copy-start | bytes 786436

commit v3 on v2

v3 whole, which is shorter than its diff:
```python
import functools

import jax
import jax.numpy as jnp
from jax import lax
from jax.experimental import pallas as pl
from jax.experimental.pallas import tpu as pltpu
from jax.sharding import PartitionSpec as P

VMEM = pltpu.VMEM
VMEM_LIMIT = 56 * 1024 * 1024


def divisor_at_most(count, most):
    return max(part for part in range(1, most + 1) if count % part == 0)


def tile_sums(group, tile_at, rows_ref, tiles_ref, into_ref, from_ref, totals):
    for local in range(group):
        place = tile_at + local
        product = jnp.dot(
            tiles_ref[local], rows_ref[from_ref[place]], preferred_element_type=jnp.float32
        )
        totals[local % len(totals)][into_ref[place]] += product


def encode_kernel(group, source_ref, slot_ref, message_ref, tiles_ref, out_ref, *totals):
    step = pl.program_id(0)

    @pl.when(step == 0)
    def _():
        for total in totals:
            total[...] = jnp.zeros_like(total)

    tile_sums(group, step * group, message_ref, tiles_ref, slot_ref, source_ref, totals)

    @pl.when(step == pl.num_programs(0) - 1)
    def _():
        out_ref[...] = sum(total[...] for total in totals).astype(out_ref.dtype)


def decode_kernel(
    group, slot_ref, target_ref, grid_hbm, rows_ref, tiles_ref, out_ref, grid_ref, load_sem, *totals
):
    step = pl.program_id(0)
    load = pltpu.make_async_copy(grid_hbm, grid_ref, load_sem)

    @pl.when(step == 0)
    def _():
        load.start()
        for total in totals:
            total[...] = jnp.zeros_like(total)

    tile_sums(group, step * group, rows_ref, tiles_ref, target_ref, slot_ref, totals)

    @pl.when(step == pl.num_programs(0) - 1)
    def _():
        load.wait()
        summed = sum(total[...] for total in totals)
        out_ref[...] = (grid_ref[...].astype(jnp.float32) + summed).astype(out_ref.dtype)


def whole(array):
    return pl.BlockSpec(array.shape, lambda step, *_: (0,) * array.ndim)


def encode(message_blocks, tiles, source, slot, slots):
    count, edge, _ = tiles.shape
    width = message_blocks.shape[2]
    group = divisor_at_most(count, 48)
    out = jax.ShapeDtypeStruct((slots, edge, width), jnp.bfloat16)
    return pl.pallas_call(
        functools.partial(encode_kernel, group),
        out_shape=out,
        grid_spec=pltpu.PrefetchScalarGridSpec(
            num_scalar_prefetch=2,
            grid=(count // group,),
            in_specs=[
                whole(message_blocks),
                pl.BlockSpec((group, edge, edge), lambda step, *_: (step, 0, 0)),
            ],
            out_specs=whole(out),
            scratch_shapes=[VMEM((slots, edge, width), jnp.float32)] * 1,
        ),
        compiler_params=pltpu.CompilerParams(vmem_limit_bytes=VMEM_LIMIT),
        name="encode",
    )(source, slot, message_blocks, tiles)


def decode(grid_blocks, rows, tiles, slot, target):
    count, edge, _ = tiles.shape
    group = divisor_at_most(count, 48)
    return pl.pallas_call(
        functools.partial(decode_kernel, group),
        out_shape=jax.ShapeDtypeStruct(grid_blocks.shape, jnp.bfloat16),
        grid_spec=pltpu.PrefetchScalarGridSpec(
            num_scalar_prefetch=2,
            grid=(count // group,),
            in_specs=[
                pl.BlockSpec(memory_space=pl.ANY),
                whole(rows),
                pl.BlockSpec((group, edge, edge), lambda step, *_: (step, 0, 0)),
            ],
            out_specs=whole(grid_blocks),
            scratch_shapes=[VMEM(grid_blocks.shape, jnp.bfloat16), pltpu.SemaphoreType.DMA]
            + [VMEM(grid_blocks.shape, jnp.float32)] * 1,
        ),
        compiler_params=pltpu.CompilerParams(vmem_limit_bytes=VMEM_LIMIT),
        name="decode",
    )(slot, target, grid_blocks, rows, tiles)


def silu(value):
    return value / (1.0 + jnp.exp(-value))


def push(source, target, send_sem, recv_sem, device):
    return pltpu.make_async_remote_copy(
        src_ref=source,
        dst_ref=target,
        send_sem=send_sem,
        recv_sem=recv_sem,
        device_id=device,
        device_id_type=pl.DeviceIdType.MESH,
    )


def matmul(left, right):
    return jnp.dot(left, right, preferred_element_type=jnp.float32)


def message_kernel(parts, grid_hbm, weight_ref, out_ref, own, other, load_sem, send_sem, recv_sem):
    me = lax.axis_index("mp")
    peer = 1 - me
    rows = own.shape[0] // parts
    half = own.shape[1]

    def part(ref, at):
        return ref.at[pl.ds(at * rows, rows)]

    loads = [
        pltpu.make_async_copy(part(grid_hbm, at), part(own, at), load_sem.at[at])
        for at in range(parts)
    ]
    for load in loads:
        load.start()
    barrier = pltpu.get_barrier_semaphore()
    pl.semaphore_signal(
        barrier, inc=1, device_id={"mp": peer}, device_id_type=pl.DeviceIdType.MESH
    )
    pl.semaphore_wait(barrier, 1)
    sends = [
        push(part(grid_hbm, at), part(other, at), send_sem.at[at], recv_sem.at[at], {"mp": peer})
        for at in range(parts)
    ]
    for send in sends:
        send.start()
    own_weight = weight_ref[pl.ds(pl.multiple_of(me * half, half), half), :]
    other_weight = weight_ref[pl.ds(pl.multiple_of(peer * half, half), half), :]
    for at in range(parts):
        loads[at].wait()
        sends[at].wait_recv()
        span = pl.ds(at * rows, rows)
        total = matmul(own[span, :], own_weight) + matmul(other[span, :], other_weight)
        out_ref[span, :] = silu(total).astype(out_ref.dtype)
    for send in sends:
        send.wait_send()


def messages(grid_nodes, send_weight):
    rows, half = grid_nodes.shape
    parts = 8
    return pl.pallas_call(
        functools.partial(message_kernel, parts),
        out_shape=jax.ShapeDtypeStruct((rows, send_weight.shape[1]), jnp.bfloat16),
        in_specs=[pl.BlockSpec(memory_space=pl.ANY), pl.BlockSpec(memory_space=VMEM)],
        out_specs=pl.BlockSpec(memory_space=VMEM),
        scratch_shapes=[VMEM((rows, half), jnp.bfloat16)] * 2
        + [pltpu.SemaphoreType.DMA((parts,))] * 3,
        compiler_params=pltpu.CompilerParams(
            collective_id=0, has_side_effects=True, vmem_limit_bytes=VMEM_LIMIT
        ),
        name="messages",
    )(grid_nodes, send_weight)


def node_kernel(
    chunks, sums_ref, linked_ref, mesh_ref, self_ref, pooled_weight_ref, out_weight_ref,
    state_ref, returned_ref,
    link_out, link_in, arrived, mesh_other, weight_own, weight_out, weight_other, pooled, pooled_other,
    hidden, hidden_other, inner, total, stage,
    link_send, link_recv, sum_send, sum_recv, back_send, back_recv, mp_send, mp_recv,
):
    bands = sums_ref.shape[0]
    blocks, edge, half = mesh_ref.shape
    part = edge // chunks
    flat = (blocks * part, half)

    def rows_of(chunk):
        return pl.ds(chunk * part, part)

    def hop_at(turn):
        return 1 + lax.rem(turn + bands // 2 - 1, bands - 1)
    me = lax.axis_index("band")
    core = lax.axis_index("mp")
    peer = 1 - core
    across = {"mp": peer}
    mine = pl.multiple_of(core * half, half)
    theirs = pl.multiple_of(peer * half, half)

    barrier = pltpu.get_barrier_semaphore()

    def greet(hop, carry):
        pl.semaphore_signal(
            barrier,
            inc=1,
            device_id={"band": lax.rem(me + hop, bands)},
            device_id_type=pl.DeviceIdType.MESH,
        )
        return carry

    lax.fori_loop(1, bands, greet, 0)
    pl.semaphore_signal(barrier, inc=1, device_id=across, device_id_type=pl.DeviceIdType.MESH)

    def spread(patch, carry):
        link_out[patch] = jnp.full(link_out.shape[1:], linked_ref[0, patch], jnp.int32)
        return carry

    lax.fori_loop(0, bands, spread, 0)
    pl.semaphore_wait(barrier, bands)

    def link_copy(patch):
        return push(
            link_out.at[patch], link_in.at[me], link_send.at[patch], link_recv.at[me],
            {"band": patch},
        )

    def sum_copy(chunk, patch, sender):
        return push(
            sums_ref.at[patch, rows_of(chunk)],
            arrived.at[sender, rows_of(chunk)],
            sum_send.at[chunk, patch],
            sum_recv.at[chunk, sender],
            {"band": patch},
        )

    def back_copy(chunk, band, sender):
        return push(
            stage.at[band, rows_of(chunk)],
            returned_ref.at[sender, rows_of(chunk)],
            back_send.at[chunk, band],
            back_recv.at[chunk, sender],
            {"band": band},
        )

    def send_links(hop, carry):
        link_copy(lax.rem(me + hop, bands)).start()
        return carry

    lax.fori_loop(1, bands, send_links, 0)
    for chunk in range(chunks):

        def send_sums(turn, carry, chunk=chunk):
            sum_copy(chunk, lax.rem(me + hop_at(turn), bands), me).start()
            return carry

        lax.fori_loop(0, bands - 1, send_sums, 0)

    mesh_copy = push(mesh_ref, mesh_other, mp_send.at[0], mp_recv.at[0], across)
    mesh_copy.start()
    weight_copies = [
        push(
            weight_out.at[which],
            weight_other.at[which],
            mp_send.at[1 + which],
            mp_recv.at[1 + which],
            across,
        )
        for which in range(2)
    ]
    for which in range(2):
        plane = out_weight_ref[:, which, :]
        swap = core == 0
        weight_own[which] = jnp.where(swap, plane[:, :half], plane[:, half:])
        weight_out[which] = jnp.where(swap, plane[:, half:], plane[:, :half])
        weight_copies[which].start()

    inner[...] = matmul(
        mesh_ref[...].reshape(blocks * edge, half), self_ref[pl.ds(mine, half), :]
    ).reshape(inner.shape)
    mesh_copy.wait()
    inner[...] += matmul(
        mesh_other[...].reshape(blocks * edge, half), self_ref[pl.ds(theirs, half), :]
    ).reshape(inner.shape)
    for copy in weight_copies:
        copy.wait()
    own_link = link_out[me, 0:1, :]

    for chunk in range(chunks):
        rows = rows_of(chunk)
        own = sums_ref[me, rows, :].astype(jnp.float32)
        for block in range(blocks):
            total[block] = jnp.where(own_link == block, own, 0.0)

        def gather(turn, carry, chunk=chunk, rows=rows):
            band = lax.rem(me + bands - hop_at(turn), bands)
            if chunk == 0:
                push(
                    link_out.at[band], link_in.at[band], link_send.at[band],
                    link_recv.at[band], {"band": band},
                ).wait_recv()
            sum_copy(chunk, band, band).wait_recv()
            value = arrived[band, rows, :].astype(jnp.float32)
            link = link_in[band, 0:1, :]
            for block in range(blocks):
                total[block] += jnp.where(link == block, value, 0.0)
            return carry

        lax.fori_loop(0, bands - 1, gather, 0)

        pooled[chunk] = total[...].reshape(flat).astype(pooled.dtype)
        pooled_copy = push(
            pooled.at[chunk], pooled_other.at[chunk],
            mp_send.at[3 + chunk], mp_recv.at[3 + chunk], across,
        )
        pooled_copy.start()
        before = inner[:, rows, :].reshape(flat) + matmul(
            pooled[chunk], pooled_weight_ref[pl.ds(mine, half), :]
        )
        pooled_copy.wait()
        before += matmul(pooled_other[chunk], pooled_weight_ref[pl.ds(theirs, half), :])
        hidden[chunk] = silu(before).astype(hidden.dtype)
        hidden_copy = push(
            hidden.at[chunk], hidden_other.at[chunk],
            mp_send.at[3 + chunks + chunk], mp_recv.at[3 + chunks + chunk], across,
        )
        hidden_copy.start()
        source = matmul(hidden[chunk], weight_own[1])
        residual = matmul(hidden[chunk], weight_own[0])
        hidden_copy.wait()
        source += matmul(hidden_other[chunk], weight_other[1])
        total[...] = source.astype(jnp.bfloat16).astype(jnp.float32).reshape(total.shape)

        def picked(link):
            value = total[0]
            for block in range(1, blocks):
                value = jnp.where(link == block, total[block], value)
            return value.astype(stage.dtype)

        def send_back(turn, carry, chunk=chunk, rows=rows, picked=picked):
            band = lax.rem(me + hop_at(turn), bands)
            stage[band, rows, :] = picked(link_in[band, 0:1, :])
            back_copy(chunk, band, me).start()
            return carry

        lax.fori_loop(0, bands - 1, send_back, 0)
        returned_ref[me, rows, :] = picked(own_link)
        residual += matmul(hidden_other[chunk], weight_other[0])
        state_ref[:, rows, :] = (
            mesh_ref[:, rows, :].astype(jnp.float32) + residual.reshape(total.shape)
        ).astype(state_ref.dtype)

    def finish(turn, carry):
        band = lax.rem(me + bands - hop_at(turn), bands)
        link_copy(band).wait_send()
        for chunk in range(chunks):
            back_copy(chunk, band, band).wait_recv()
            sum_copy(chunk, band, me).wait_send()
            back_copy(chunk, band, me).wait_send()
        return carry

    lax.fori_loop(0, bands - 1, finish, 0)


def update_nodes(sums, linked, mesh_nodes, self_weight, pooled_weight, out_weight):
    bands, edge, half = sums.shape
    mesh_blocks = mesh_nodes.reshape(-1, edge, half)
    blocks = mesh_blocks.shape[0]
    chunks = 2
    nodes = VMEM((chunks, blocks * edge // chunks, half), jnp.bfloat16)
    by_band = pltpu.SemaphoreType.DMA((bands,))
    by_part = pltpu.SemaphoreType.DMA((chunks, bands))
    by_use = pltpu.SemaphoreType.DMA((3 + 2 * chunks,))
    vmem = pl.BlockSpec(memory_space=VMEM)
    state, returned = pl.pallas_call(
        functools.partial(node_kernel, chunks),
        out_shape=(
            jax.ShapeDtypeStruct(mesh_blocks.shape, jnp.bfloat16),
            jax.ShapeDtypeStruct(sums.shape, jnp.bfloat16),
        ),
        in_specs=[vmem, pl.BlockSpec(memory_space=pltpu.SMEM)] + [vmem] * 4,
        out_specs=(vmem, vmem),
        scratch_shapes=[
            VMEM((bands, 8, half), jnp.int32),
            VMEM((bands, 8, half), jnp.int32),
            VMEM(sums.shape, jnp.bfloat16),
            VMEM(mesh_blocks.shape, jnp.bfloat16),
            VMEM((2, out_weight.shape[0], half), jnp.bfloat16),
            VMEM((2, out_weight.shape[0], half), jnp.bfloat16),
            VMEM((2, out_weight.shape[0], half), jnp.bfloat16),
            nodes,
            nodes,
            nodes,
            nodes,
            VMEM(mesh_blocks.shape, jnp.float32),
            VMEM((blocks, edge // chunks, half), jnp.float32),
            VMEM(sums.shape, jnp.bfloat16),
        ]
        + [by_band] * 2
        + [by_part] * 4
        + [by_use] * 2,
        compiler_params=pltpu.CompilerParams(
            collective_id=1, has_side_effects=True, vmem_limit_bytes=VMEM_LIMIT
        ),
        name="update_nodes",
    )(sums, linked, mesh_blocks, self_weight, pooled_weight, out_weight)
    return state.reshape(mesh_nodes.shape), returned


def per_device(
    grid_nodes,
    mesh_nodes,
    send_weight,
    self_weight,
    pooled_weight,
    out_weight,
    encode_source,
    encode_slot,
    encode_tiles,
    slot_block,
    decode_slot,
    decode_target,
    decode_tiles,
):
    band_count = lax.axis_size("band")
    tile_edge = encode_tiles.shape[1]
    feature_width = grid_nodes.shape[1]
    grid_blocks = grid_nodes.shape[0] // tile_edge
    message = messages(grid_nodes, send_weight)
    message_blocks = message.reshape(grid_blocks, tile_edge, feature_width)
    slot_sums = encode(message_blocks, encode_tiles, encode_source, encode_slot, band_count)
    mesh_state, returned = update_nodes(
        slot_sums, slot_block, mesh_nodes, self_weight, pooled_weight, out_weight
    )
    grid_state = decode(
        grid_nodes.reshape(grid_blocks, tile_edge, feature_width),
        returned,
        decode_tiles,
        decode_slot,
        decode_target,
    ).reshape(grid_nodes.shape)
    return (grid_state, mesh_state)


def solution(mesh):
    return jax.shard_map(
        per_device,
        mesh=mesh,
        in_specs=(
            P("band", "mp"),
            P("band", "mp"),
            P(None, "mp"),
            P(None, "mp"),
            P(None, "mp"),
            P("mp", None, None),
            P("band"),
            P("band"),
            P("band", None, None),
            P("band", None),
            P("band"),
            P("band"),
            P("band", None, None),
        ),
        out_specs=(P("band", "mp"), P("band", "mp")),
        check_vma=False,
    )
```

time: 95.2 us -> 87.9 us (0.923)
  the two profiles are of different devices: /device:TPU:30 before, /device:TPU:8 now
where the time goes in v3:
time: 87.9 us; the launch traced here: 86.2 us
  Pallas kernels  84.8 us (96%)
    pallas_call x1, Pallas kernels, update_nodes(): pl.pallas_call(functools.partial(node_kernel, chunks), out_shape=(jax.Sha...  59.5 us
    pallas_call x1, Pallas kernels, decode(): pl.pallas_call(functools.partial(decode_kernel, group), out_shape=jax.Sha...  9 us
    pallas_call x1, Pallas kernels, encode(): pl.pallas_call(functools.partial(encode_kernel, group), out_shape=out, gr...  8.49 us
    pallas_call x1, Pallas kernels, messages(): pl.pallas_call(functools.partial(message_kernel, parts), out_shape=jax.Sh...  7.8 us

profile of v3, /device:TPU:8, one launch (start us, length us, event | category | flops | bytes accessed | tf_op | source)
XLA Modules:
  0.0 86.2 jit_solution(13833891469558230600)
XLA Ops:
  0.6 7.8 %messages.1 = bf16[4096,256]{1,0:T(8,128)(2,1)} custom-call(bf16[4096,256]{1,0:T(8,128)(2,1)} %grid_hbm.1, bf16[512,256]{1,0:T(8,128)(2,1)} %weight_ref.1), custom_call_target="tpu_custom_call" | custom-call | tf_op jit(solution)/shard_map/messages/pallas_call | solution.py:173
  8.4 8.5 %encode.1.sums_ref = bf16[16,128,256]{2,1,0:T(8,128)(2,1)} custom-call(s32[192]{0:T(256)} %source_ref.1, s32[192]{0:T(256)} %slot_ref.2, bf16[32,128,256]{2,1,0:T(8,128)(2,1)} %bitcast.5, bf16[192,128,128]{2,1,0:T(8,128)(2,1)} %tiles_ref.2), custom_call_target="tpu_custom_call" | custom-call | tf_op jit(solution)/shard_map/encode/pallas_call | solution.py:72
  16.9 59.5 %update_nodes.1 = (bf16[4,128,256]{2,1,0:T(8,128)(2,1)}, bf16[16,128,256]{2,1,0:T(8,128)(2,1)}) custom-call(bf16[16,128,256]{2,1,0:T(8,128)(2,1)} %encode.1.sums_ref, s32[1,16]{1,0:T(1,128)} %linked_ref.1, bf16[4,128,256]{2,1,0:T(8,128)(2,1)} %bitcast.8, bf16[512,256]{1,0:T(8,128)(2,1)} %self_ref.1, bf16[512,256]{1,0:T(8,128)(2,1)} %pooled_weight_ref.1, ...), custom_call_target="tpu_custom_call" | custom-call | tf_op jit(solution)/shard_map/update_nodes/pallas_call | solution.py:385
  76.5 0.0 copy-start
  76.5 9.0 %decode.1 = bf16[32,128,256]{2,1,0:T(8,128)(2,1)} custom-call(s32[192]{0:T(256)} %slot_ref.3, s32[192]{0:T(256)} %target_ref.1, bf16[32,128,256]{2,1,0:T(8,128)(2,1)} %bitcast.6, bf16[16,128,256]{2,1,0:T(8,128)(2,1)} %get-tuple-element.4.rows_ref, bf16[192,128,128]{2,1,0:T(8,128)(2,1)} %tiles_ref.3), custom_call_target="tpu_custom_call" | custom-call | tf_op jit(solution)/shard_map/decode/pallas_call | solution.py:93
  85.5 0.0 copy-done
  85.5 0.7 copy.16
Async XLA Ops:
  76.5 9.0 %copy-start = (bf16[4,128,256]{2,1,0:T(8,128)(2,1)S(1)}, bf16[4,128,256]{2,1,0:T(8,128)(2,1)}, u32[]{:S(2)}) copy-start(bf16[4,128,256]{2,1,0:T(8,128)(2,1)} %get-tuple-element.5) | copy-start | bytes 786436

commit v4 on v3

--- a/solution.py
+++ b/solution.py
@@ -67,7 +67,7 @@
 def encode(message_blocks, tiles, source, slot, slots):
     count, edge, _ = tiles.shape
     width = message_blocks.shape[2]
-    group = divisor_at_most(count, 48)
+    group = divisor_at_most(count, 96)
     out = jax.ShapeDtypeStruct((slots, edge, width), jnp.bfloat16)
     return pl.pallas_call(
         functools.partial(encode_kernel, group),
@@ -89,7 +89,7 @@
 
 def decode(grid_blocks, rows, tiles, slot, target):
     count, edge, _ = tiles.shape
-    group = divisor_at_most(count, 48)
+    group = divisor_at_most(count, 96)
     return pl.pallas_call(
         functools.partial(decode_kernel, group),
         out_shape=jax.ShapeDtypeStruct(grid_blocks.shape, jnp.bfloat16),
@@ -169,7 +169,7 @@
 
 def messages(grid_nodes, send_weight):
     rows, half = grid_nodes.shape
-    parts = 8
+    parts = 4
     return pl.pallas_call(
         functools.partial(message_kernel, parts),
         out_shape=jax.ShapeDtypeStruct((rows, send_weight.shape[1]), jnp.bfloat16),
@@ -200,7 +200,7 @@
         return pl.ds(chunk * part, part)
 
     def hop_at(turn):
-        return 1 + lax.rem(turn + bands // 2 - 1, bands - 1)
+        return 1 + turn
     me = lax.axis_index("band")
     core = lax.axis_index("mp")
     peer = 1 - core

time: 87.9 us -> 83.9 us (0.954)
  Pallas kernels: 84.8 us -> 81 us
    pallas_call x1, Pallas kernels: 59.5 us -> 56.8 us  [update_nodes(): pl.pallas_call(functools.partial(node_kernel, chunks), out_shape=(jax.Sha...]
where the time goes in v4:
time: 83.9 us; the launch traced here: 82.4 us
  Pallas kernels  81 us (97%)
    pallas_call x1, Pallas kernels, update_nodes(): pl.pallas_call(functools.partial(node_kernel, chunks), out_shape=(jax.Sha...  56.8 us
    pallas_call x1, Pallas kernels, decode(): pl.pallas_call(functools.partial(decode_kernel, group), out_shape=jax.Sha...  8.59 us
    pallas_call x1, Pallas kernels, encode(): pl.pallas_call(functools.partial(encode_kernel, group), out_shape=out, gr...  8.1 us
    pallas_call x1, Pallas kernels, messages(): pl.pallas_call(functools.partial(message_kernel, parts), out_shape=jax.Sh...  7.49 us

profile of v4, /device:TPU:8, one launch (start us, length us, event | category | flops | bytes accessed | tf_op | source)
XLA Modules:
  0.0 82.4 jit_solution(10355766429308678891)
XLA Ops:
  0.6 7.5 %messages.1 = bf16[4096,256]{1,0:T(8,128)(2,1)} custom-call(bf16[4096,256]{1,0:T(8,128)(2,1)} %grid_hbm.1, bf16[512,256]{1,0:T(8,128)(2,1)} %weight_ref.1), custom_call_target="tpu_custom_call" | custom-call | tf_op jit(solution)/shard_map/messages/pallas_call | solution.py:173
  8.1 8.1 %encode.1.sums_ref = bf16[16,128,256]{2,1,0:T(8,128)(2,1)} custom-call(s32[192]{0:T(256)} %source_ref.1, s32[192]{0:T(256)} %slot_ref.2, bf16[32,128,256]{2,1,0:T(8,128)(2,1)} %bitcast.5, bf16[192,128,128]{2,1,0:T(8,128)(2,1)} %tiles_ref.2), custom_call_target="tpu_custom_call" | custom-call | tf_op jit(solution)/shard_map/encode/pallas_call | solution.py:72
  16.2 56.8 %update_nodes.1 = (bf16[4,128,256]{2,1,0:T(8,128)(2,1)}, bf16[16,128,256]{2,1,0:T(8,128)(2,1)}) custom-call(bf16[16,128,256]{2,1,0:T(8,128)(2,1)} %encode.1.sums_ref, s32[1,16]{1,0:T(1,128)} %linked_ref.1, bf16[4,128,256]{2,1,0:T(8,128)(2,1)} %bitcast.8, bf16[512,256]{1,0:T(8,128)(2,1)} %self_ref.1, bf16[512,256]{1,0:T(8,128)(2,1)} %pooled_weight_ref.1, ...), custom_call_target="tpu_custom_call" | custom-call | tf_op jit(solution)/shard_map/update_nodes/pallas_call | solution.py:385
  73.1 0.0 copy-start
  73.1 8.6 %decode.1 = bf16[32,128,256]{2,1,0:T(8,128)(2,1)} custom-call(s32[192]{0:T(256)} %slot_ref.3, s32[192]{0:T(256)} %target_ref.1, bf16[32,128,256]{2,1,0:T(8,128)(2,1)} %bitcast.6, bf16[16,128,256]{2,1,0:T(8,128)(2,1)} %get-tuple-element.4.rows_ref, bf16[192,128,128]{2,1,0:T(8,128)(2,1)} %tiles_ref.3), custom_call_target="tpu_custom_call" | custom-call | tf_op jit(solution)/shard_map/decode/pallas_call | solution.py:93
  81.7 0.0 copy-done
  81.7 0.7 copy.16
Async XLA Ops:
  73.1 8.6 %copy-start = (bf16[4,128,256]{2,1,0:T(8,128)(2,1)S(1)}, bf16[4,128,256]{2,1,0:T(8,128)(2,1)}, u32[]{:S(2)}) copy-start(bf16[4,128,256]{2,1,0:T(8,128)(2,1)} %get-tuple-element.5) | copy-start | bytes 786436
